TPU v7x, 256 devices: a whole 4x4x8 slice. The times are simulated.
256 devices in a mesh: row: 32 (over z, x), col: 8 (over y, core).
Axes of the slice: x: 4, y: 4, z: 8, core: 2. Of those that a mesh axis runs over, the one named last changes fastest.
Arguments:
- right_sides: bfloat16 [4, 512, 32, 256], P(None, 'row', 'col'), may hold values from -6 to 6
- lower_blocks: bfloat16 [6, 32, 32, 256, 256], P(None, 'col', 'row'), may hold values from -0.21875 to 0.21875
- lower_fill: int32 [6, 32, 32], P(None, 'col', 'row'), may hold values from 0 to 1, as said below
- upper_blocks: bfloat16 [6, 32, 32, 256, 256], P(None, 'col', 'row'), may hold values from -0.21875 to 0.21875
- upper_fill: int32 [6, 32, 32], P(None, 'col', 'row'), may hold values from 0 to 1, as said below
- lower_inv: bfloat16 [4, 32, 256, 256], P(None, 'col')
- upper_inv: bfloat16 [4, 32, 256, 256], P(None, 'col')
Outputs:
- solution: float32 [4, 512, 32, 256], P(None, 'row', 'col')
Inputs may be any that keep to these rules, and one draw needn't show every extreme that they name: The fill follows an elimination forest: each supernode of a level below the top has one parent on the next level; lower_fill at [a (a - 1) / 2 + b, i, j] is 1 exactly when supernode i of level a is the ancestor of supernode j of level b, else 0. The same forest as lower_fill with the two supernode indices swapped: upper_fill at [a (a - 1) / 2 + b, i, j] is 1 exactly when supernode j of level a is the ancestor of supernode i of level b.
All inputs are finite; a program needn't handle non-finite values.
Results may differ from a plain program's by a relative error of at most 0.007.
Values may be sent and summed in bfloat16 or wider, within the bound.
A program may use at most 64 MiB of HBM per device.

v0:
```python
import jax
import jax.numpy as jnp
from jax import lax
from jax.sharding import PartitionSpec as P


def spread(x, axis, root):
    mine = lax.axis_index(axis) == root
    return lax.psum(jnp.where(mine, x, jnp.zeros_like(x)), axis)


def pair_index(current, earlier):
    upper_level = max(current, earlier)
    lower_level = min(current, earlier)
    return upper_level * (upper_level - 1) // 2 + lower_level


def deliver(solved_local):
    gathered = lax.all_gather(solved_local, "row", axis=0, tiled=True)
    row_place = lax.axis_index("row")
    targets_here = gathered.shape[1]
    selected = lax.dynamic_slice_in_dim(gathered, row_place % targets_here, 1, 1)
    arrived = spread(selected, "col", row_place // targets_here)
    return arrived[:, 0, :]


def triangular_sweep(right_sides, blocks, fills, inverses, level_order):
    local_rows = right_sides.shape[1]
    targets_here = right_sides.shape[2]
    width = right_sides.shape[3]
    solved = [None] * len(level_order)
    sources = {}
    finished = []
    for position, current in enumerate(level_order):
        if finished:
            operands = []
            for earlier in finished:
                which = pair_index(current, earlier)
                operands.append(
                    (sources[earlier], blocks[which][:, 0], fills[which][:, 0].astype(jnp.float32))
                )

            def partial_terms(first_row, row_count, operands=operands):
                running = jnp.zeros((row_count, targets_here, width), jnp.float32)
                for solution_rows, block_tiles, fill_mask in operands:
                    product = jnp.einsum(
                        "rv,tvw->rtw",
                        solution_rows,
                        block_tiles,
                        preferred_element_type=jnp.float32,
                    )
                    running = running + product * fill_mask[None, :, None]
                return running

            level_sums = lax.psum_scatter(
                partial_terms(jnp.int32(0), local_rows * lax.axis_size("row")),
                "row",
                scatter_dimension=0,
                tiled=True,
            )
            residual = (right_sides[current].astype(jnp.float32) - level_sums).astype(jnp.bfloat16)
        else:
            residual = right_sides[current]
        solved_block = jnp.einsum(
            "rtv,tvw->rtw", residual, inverses[current], preferred_element_type=jnp.float32
        )
        solved[current] = solved_block
        if position + 1 < len(level_order):
            delivered = deliver(solved_block.astype(jnp.bfloat16))
            sources[current] = delivered
        finished.append(current)
    return solved


def per_device(
    right_sides, lower_blocks, lower_fill, upper_blocks, upper_fill, lower_inv, upper_inv
):
    levels = right_sides.shape[0]
    forward = triangular_sweep(
        right_sides, lower_blocks, lower_fill, lower_inv, list(range(levels))
    )
    middle = jnp.stack([block.astype(jnp.bfloat16) for block in forward])
    backward = triangular_sweep(
        middle, upper_blocks, upper_fill, upper_inv, list(range(levels - 1, -1, -1))
    )
    return jnp.stack(backward)


def solution(mesh):
    placed = (
        P(None, "row", "col", None),
        P(None, "col", "row", None, None),
        P(None, "col", "row"),
        P(None, "col", "row", None, None),
        P(None, "col", "row"),
        P(None, "col", None, None),
        P(None, "col", None, None),
    )
    return jax.shard_map(
        per_device,
        mesh=mesh,
        in_specs=placed,
        out_specs=P(None, "row", "col", None),
        check_vma=False,
    )
```

profile of v0, /device:TPU:1, one launch (start us, length us, event | category | flops | bytes accessed | tf_op | source)
XLA Modules:
  0.0 1977.9 jit_solution(1539664762007637912)
XLA Ops:
  9.2 71.4 %all-gather.7.cloned.1.call-done = bf16[512,4,256]{2,0,1:T(8,128)(2,1)} async-done(((bf16[16,4,256]{2,0,1:T(8,128)(2,1)}), bf16[512,4,256]{2,0,1:T(8,128)(2,1)}) %all-gather.7.cloned.1.call-update) | async-done | bytes 1048592 | tf_op jit(solution)/shard_map/all_gather | solution.py:19
  83.5 65.4 %all-reduce.13.cloned.1.call-done = bf16[512,256]{1,0:T(8,128)(2,1)} async-done(((bf16[512,256]{1,0:T(8,128)(2,1)}), bf16[512,256]{1,0:T(8,128)(2,1)}) %all-reduce.13.cloned.1.call-update) | async-done | bytes 262160 | tf_op jit(solution)/shard_map/psum | solution.py:9
  150.4 2.6 copy.19
  155.0 149.2 %all-reduce.25.cloned.1.call-done = f32[512,4,256]{2,1,0:T(4,128)} async-done(((f32[512,4,256]{2,1,0:T(4,128)}), f32[512,4,256]{2,1,0:T(4,128)}) %all-reduce.25.cloned.1.call-update) | async-done | bytes 2097168
  307.0 68.6 %all-gather.9.cloned.1.call-done = bf16[512,4,256]{2,0,1:T(8,128)(2,1)} async-done(((bf16[16,4,256]{2,0,1:T(8,128)(2,1)}), bf16[512,4,256]{2,0,1:T(8,128)(2,1)}) %all-gather.9.cloned.1.call-update) | async-done | bytes 1048592 | tf_op jit(solution)/shard_map/all_gather | solution.py:19
  378.8 64.8 %all-reduce.15.cloned.1.call-done = bf16[512,256]{1,0:T(8,128)(2,1)} async-done(((bf16[512,256]{1,0:T(8,128)(2,1)}), bf16[512,256]{1,0:T(8,128)(2,1)}) %all-reduce.15.cloned.1.call-update) | async-done | bytes 262160 | tf_op jit(solution)/shard_map/psum | solution.py:9
  447.9 151.1 %all-reduce.27.cloned.1.call-done = f32[512,4,256]{2,1,0:T(4,128)} async-done(((f32[512,4,256]{2,1,0:T(4,128)}), f32[512,4,256]{2,1,0:T(4,128)}) %all-reduce.27.cloned.1.call-update) | async-done | bytes 2097168
  603.3 67.1 %all-gather.11.cloned.1.call-done = bf16[512,4,256]{2,0,1:T(8,128)(2,1)} async-done(((bf16[16,4,256]{2,0,1:T(8,128)(2,1)}), bf16[512,4,256]{2,0,1:T(8,128)(2,1)}) %all-gather.11.cloned.1.call-update) | async-done | bytes 1048592 | tf_op jit(solution)/shard_map/all_gather | solution.py:19
  672.1 2.8 fusion.9
  675.0 63.6 %all-reduce.17.cloned.1.call-done = bf16[512,256]{1,0:T(8,128)(2,1)} async-done(((bf16[512,256]{1,0:T(8,128)(2,1)}), bf16[512,256]{1,0:T(8,128)(2,1)}) %all-reduce.17.cloned.1.call-update) | async-done | bytes 262160 | tf_op jit(solution)/shard_map/psum | solution.py:9
  743.7 151.1 %all-reduce.29.cloned.1.call-done = f32[512,4,256]{2,1,0:T(4,128)} async-done(((f32[512,4,256]{2,1,0:T(4,128)}), f32[512,4,256]{2,1,0:T(4,128)}) %all-reduce.29.cloned.1.call-update) | async-done | bytes 2097168
  897.7 68.6 %all-gather.13.cloned.1.call-done = bf16[512,4,256]{2,0,1:T(8,128)(2,1)} async-done(((bf16[16,4,256]{2,0,1:T(8,128)(2,1)}), bf16[512,4,256]{2,0,1:T(8,128)(2,1)}) %all-gather.13.cloned.1.call-update) | async-done | bytes 1048592 | tf_op jit(solution)/shard_map/all_gather | solution.py:19
  968.2 66.3 %all-reduce.19.cloned.1.call-done = bf16[512,256]{1,0:T(8,128)(2,1)} async-done(((bf16[512,256]{1,0:T(8,128)(2,1)}), bf16[512,256]{1,0:T(8,128)(2,1)}) %all-reduce.19.cloned.1.call-update) | async-done | bytes 262160 | tf_op jit(solution)/shard_map/psum | solution.py:9
  1034.5 2.9 convolution_multiply_fusion
  1037.5 214.5 %reduce-scatter.4.cloned.1.call-done = f32[16,4,256]{2,0,1:T(8,128)} async-done(((f32[512,4,256]{2,0,1:T(8,128)}), f32[16,4,256]{2,0,1:T(8,128)}) %reduce-scatter.4.cloned.1.call-update) | async-done | bytes 65552 | tf_op jit(solution)/shard_map/reduce_scatter | solution.py:55
  1253.7 71.2 %all-gather.15.cloned.1.call-done = bf16[512,4,256]{2,0,1:T(8,128)(2,1)} async-done(((bf16[16,4,256]{2,0,1:T(8,128)(2,1)}), bf16[512,4,256]{2,0,1:T(8,128)(2,1)}) %all-gather.15.cloned.1.call-update) | async-done | bytes 1048592 | tf_op jit(solution)/shard_map/all_gather | solution.py:19
  1328.1 64.8 %all-reduce.21.cloned.1.call-done = bf16[512,256]{1,0:T(8,128)(2,1)} async-done(((bf16[512,256]{1,0:T(8,128)(2,1)}), bf16[512,256]{1,0:T(8,128)(2,1)}) %all-reduce.21.cloned.1.call-update) | async-done | bytes 262160 | tf_op jit(solution)/shard_map/psum | solution.py:9
  1393.0 2.9 multiply_add_fusion.1
  1396.0 214.5 %reduce-scatter.6.cloned.1.call-done = f32[16,4,256]{2,0,1:T(8,128)} async-done(((f32[512,4,256]{2,0,1:T(8,128)}), f32[16,4,256]{2,0,1:T(8,128)}) %reduce-scatter.6.cloned.1.call-update) | async-done | bytes 65552 | tf_op jit(solution)/shard_map/reduce_scatter | solution.py:55
  1613.9 69.4 %all-gather.17.cloned.1.call-done = bf16[512,4,256]{2,0,1:T(8,128)(2,1)} async-done(((bf16[16,4,256]{2,0,1:T(8,128)(2,1)}), bf16[512,4,256]{2,0,1:T(8,128)(2,1)}) %all-gather.17.cloned.1.call-update) | async-done | bytes 1048592 | tf_op jit(solution)/shard_map/all_gather | solution.py:19
  1685.1 2.8 fusion.6
  1687.9 63.5 %all-reduce.23.cloned.1.call-done = bf16[512,256]{1,0:T(8,128)(2,1)} async-done(((bf16[512,256]{1,0:T(8,128)(2,1)}), bf16[512,256]{1,0:T(8,128)(2,1)}) %all-reduce.23.cloned.1.call-update) | async-done | bytes 262160 | tf_op jit(solution)/shard_map/psum | solution.py:9
  1751.4 3.7 multiply_add_fusion
  1755.1 213.8 %reduce-scatter.8.cloned.1.call-done = f32[16,4,256]{2,0,1:T(8,128)} async-done(((f32[512,4,256]{2,0,1:T(8,128)}), f32[16,4,256]{2,0,1:T(8,128)}) %reduce-scatter.8.cloned.1.call-update) | async-done | bytes 65552 | tf_op jit(solution)/shard_map/reduce_scatter | solution.py:55
  (89 shorter events, 46.7 us)
Async XLA Ops:
  6.5 74.1 %all-gather.7.cloned.1.call-start = ((), (), s32[]{:S(2)}) async-start(), calls=%async_computation.3 | async-start | bytes 1081344 | tf_op jit(solution)/shard_map/all_gather | solution.py:19
  9.2 139.7 %all-reduce.13.cloned.1.call-start = ((), (), s32[]{:S(2)}) async-start(), calls=%async_computation.4 | async-start | bytes 524288 | tf_op jit(solution)/shard_map/psum | solution.py:9
  82.3 221.9 %all-reduce.25.cloned.1.call-start = ((), (), s32[]{:S(2)}) async-start(), calls=%async_computation.18 | async-start | bytes 4194304
  153.1 224.2 %copy-start = (bf16[512,256]{1,0:T(8,128)(2,1)S(1)}, bf16[512,256]{1,0:T(8,128)(2,1)}, u32[]{:S(2)}) copy-start(bf16[512,256]{1,0:T(8,128)(2,1)} %all-reduce.13.cloned.1.call-done) | copy-start | bytes 786436
  153.1 222.4 %all-gather.9.cloned.1.call-start = ((), (), s32[]{:S(2)}) async-start(), calls=%async_computation.5 | async-start | bytes 1081344 | tf_op jit(solution)/shard_map/all_gather | solution.py:19
  306.9 136.7 %all-reduce.15.cloned.1.call-start = ((), (), s32[]{:S(2)}) async-start(), calls=%async_computation.6 | async-start | bytes 524288 | tf_op jit(solution)/shard_map/psum | solution.py:9
  377.2 221.8 %all-reduce.27.cloned.1.call-start = ((), (), s32[]{:S(2)}) async-start(), calls=%async_computation.19 | async-start | bytes 4194304
  447.9 222.5 %all-gather.11.cloned.1.call-start = ((), (), s32[]{:S(2)}) async-start(), calls=%async_computation.7 | async-start | bytes 1081344 | tf_op jit(solution)/shard_map/all_gather | solution.py:19
  601.8 136.9 %all-reduce.17.cloned.1.call-start = ((), (), s32[]{:S(2)}) async-start(), calls=%async_computation.8 | async-start | bytes 524288 | tf_op jit(solution)/shard_map/psum | solution.py:9
  672.1 222.7 %all-reduce.29.cloned.1.call-start = ((), (), s32[]{:S(2)}) async-start(), calls=%async_computation.20 | async-start | bytes 4194304
  743.6 224.4 %copy-start.9 = (s32[6,4,1]{0,2,1:T(1,128)S(1)}, s32[6,4,1]{0,2,1:T(1,128)}, u32[]{:S(2)}) copy-start(s32[6,4,1]{0,2,1:T(1,128)} %param.11) | copy-start | bytes 292
  743.7 222.6 %all-gather.13.cloned.1.call-start = ((), (), s32[]{:S(2)}) async-start(), calls=%async_computation.9 | async-start | bytes 1081344 | tf_op jit(solution)/shard_map/all_gather | solution.py:19
  897.6 136.9 %all-reduce.19.cloned.1.call-start = ((), (), s32[]{:S(2)}) async-start(), calls=%async_computation.10 | async-start | bytes 524288 | tf_op jit(solution)/shard_map/psum | solution.py:9
  967.9 284.0 %reduce-scatter.4.cloned.1.call-start = ((), (), s32[]{:S(2)}) async-start(), calls=%async_computation.11 | async-start | bytes 2162688 | tf_op jit(solution)/shard_map/reduce_scatter | solution.py:55
  1034.5 217.5 %copy-start.6 = (bf16[16,4,256]{2,0,1:T(8,128)(2,1)S(1)}, bf16[16,4,256]{2,0,1:T(8,128)(2,1)}, u32[]{:S(2)}) copy-start(bf16[16,4,256]{2,0,1:T(8,128)(2,1)} %fusion.1) | copy-start | bytes 98308
  1037.4 289.2 %copy-start.1 = (bf16[512,256]{1,0:T(8,128)(2,1)S(1)}, bf16[512,256]{1,0:T(8,128)(2,1)}, u32[]{:S(2)}) copy-start(bf16[512,256]{1,0:T(8,128)(2,1)} %all-reduce.19.cloned.1.call-done) | copy-start | bytes 786436
  1037.4 287.5 %all-gather.15.cloned.1.call-start = ((), (), s32[]{:S(2)}) async-start(), calls=%async_computation.12 | async-start | bytes 1081344 | tf_op jit(solution)/shard_map/all_gather | solution.py:19
  1253.6 139.3 %all-reduce.21.cloned.1.call-start = ((), (), s32[]{:S(2)}) async-start(), calls=%async_computation.13 | async-start | bytes 524288 | tf_op jit(solution)/shard_map/psum | solution.py:9
  1326.6 283.9 %reduce-scatter.6.cloned.1.call-start = ((), (), s32[]{:S(2)}) async-start(), calls=%async_computation.14 | async-start | bytes 2162688 | tf_op jit(solution)/shard_map/reduce_scatter | solution.py:55
  1395.9 214.6 %copy-start.5 = (bf16[16,4,256]{2,0,1:T(8,128)(2,1)S(1)}, bf16[16,4,256]{2,0,1:T(8,128)(2,1)}, u32[]{:S(2)}) copy-start(bf16[16,4,256]{2,0,1:T(8,128)(2,1)} %fusion) | copy-start | bytes 98308
  1395.9 289.1 %copy-start.3 = (bf16[512,256]{1,0:T(8,128)(2,1)S(1)}, bf16[512,256]{1,0:T(8,128)(2,1)}, u32[]{:S(2)}) copy-start(bf16[512,256]{1,0:T(8,128)(2,1)} %all-reduce.21.cloned.1.call-done) | copy-start | bytes 786436
  1395.9 287.4 %all-gather.17.cloned.1.call-start = ((), (), s32[]{:S(2)}) async-start(), calls=%async_computation.15 | async-start | bytes 1081344 | tf_op jit(solution)/shard_map/all_gather | solution.py:19
  1612.4 139.0 %all-reduce.23.cloned.1.call-start = ((), (), s32[]{:S(2)}) async-start(), calls=%async_computation.16 | async-start | bytes 524288 | tf_op jit(solution)/shard_map/psum | solution.py:9
  1685.0 283.9 %reduce-scatter.8.cloned.1.call-start = ((), (), s32[]{:S(2)}) async-start(), calls=%async_computation.17 | async-start | bytes 2162688 | tf_op jit(solution)/shard_map/reduce_scatter | solution.py:55
  (5 other events, 589.9 us)
Sparse Core Ops, SparseCore 0:
  9.8 70.7 all-gather.6
  82.9 65.8 all-reduce.12
  153.2 150.9 all-reduce.24
  307.0 68.4 all-gather.8
  377.7 65.8 all-reduce.14
  448.0 150.9 all-reduce.26
  601.9 68.4 all-gather.10
  672.7 65.8 all-reduce.16
  743.8 150.9 all-reduce.28
  897.7 68.4 all-gather.12
  968.6 65.8 all-reduce.18
  1038.7 213.2 reduce-scatter.3
  1254.4 70.4 all-gather.14
  1327.1 65.8 all-reduce.20
  1397.1 213.2 reduce-scatter.5
  1612.8 70.4 all-gather.16
  1685.5 65.8 all-reduce.22
  1755.6 213.2 reduce-scatter.7
where the time goes:
time: 1980 us
  waiting for transfers between devices  1900 us (96%)
  matrix products  38.9 us (2%)
    reduce_scatter x3, waiting for transfers between devices, triangular_sweep(): lax.psum_scatter(partial_terms(jnp.int32(0), local_rows * lax.axis_size('...  643 us
    unnamed x21, waiting for transfers between devices  452 us
    all_gather x6, waiting for transfers between devices, deliver(): gathered = lax.all_gather(solved_local, 'row', axis=0, tiled=True)  416 us
    psum x6, waiting for transfers between devices, spread(): return lax.psum(jnp.where(mine, x, jnp.zeros_like(x)), axis)  388 us
  transfers between devices with their start and end apart: 18, of which 18 were waited for; matrix products, arithmetic and copies ran while one was open for 1% of the time, Pallas kernels for 0%

commit v1 on v0

v1 whole, which is shorter than its diff:
```python
import functools

import jax
import jax.numpy as jnp
from jax import lax
from jax.experimental import pallas as pl
from jax.experimental.pallas import tpu as pltpu
from jax.sharding import PartitionSpec as P

MESH = pl.DeviceIdType.MESH
F32 = jnp.float32
BF16 = jnp.bfloat16


def pair_index(current, earlier):
    upper_level = max(current, earlier)
    lower_level = min(current, earlier)
    return upper_level * (upper_level - 1) // 2 + lower_level


def sweep_kernel(
    dims, rhs, lower, lower_fill, upper, upper_fill, lower_inv, upper_inv, out,
    l_raw, u_raw, linv, uinv, l_loc, l_in, l_sum, l_home, u_in, u_sum, u_slice, u_home,
    rhs_home, fwd, flag_out, flag_x, flag_row, flag_all, flags,
    near, part_out, part_in, solved, pick_out, pick_in, pick_own, answer,
    load_sem, inv_sem, flag_sem,
    rhs_s, rhs_r, fx_s, fx_r, fd_s, fd_r, ly_s, ly_r, ld_s, ld_r, ux_s, ux_r, uz_s, uz_r,
    ua_s, ua_r, na_s, na_r, pb_s, pb_r, xa_s, xa_r, xb_s, xb_r, out_s, out_r,
):
    lev, nx, nc, rows, width = dims
    pairs = lev * (lev - 1) // 2
    nz = nc
    step = width // nc
    row = lax.axis_index("row")
    c = lax.axis_index("col")
    z = lax.div(row, nx)
    x = lax.rem(row, nx)
    diagonal = c == z

    def wrap(value, count):
        return lax.rem(value, count)

    def send(src, dst, ssem, rsem, to_row, to_col):
        pltpu.make_async_remote_copy(
            src_ref=src, dst_ref=dst, send_sem=ssem, recv_sem=rsem,
            device_id=(to_row, to_col), device_id_type=MESH,
        ).start()

    def wait(ref, sem):
        pltpu.make_async_copy(ref, ref, sem).wait()

    def x_peer(k):
        return z * nx + wrap(x + k, nx)

    def z_peer(k):
        return wrap(z + k, nz) * nx + x

    def each(count, body):
        def run(k, carry):
            body(k)
            return carry

        lax.fori_loop(1, count, run, 0)

    order = []
    for a in range(1, lev):
        for b in range(a):
            order.append(pair_index(a, b))
    back = []
    for b in range(lev - 2, -1, -1):
        for a in range(b + 1, lev):
            back.append(pair_index(a, b))

    def load_lower(p):
        return pltpu.make_async_copy(lower.at[p, :, 0], l_raw.at[p], load_sem.at[p])

    def load_upper(p):
        return pltpu.make_async_copy(upper.at[p, :, 0], u_raw.at[p], load_sem.at[pairs + p])

    def load_linv(l):
        return pltpu.make_async_copy(lower_inv.at[l, x], linv.at[l], inv_sem.at[l])

    def load_uinv(l):
        return pltpu.make_async_copy(upper_inv.at[l, x], uinv.at[l], inv_sem.at[lev + l])

    load_lower(order[0]).start()
    load_linv(0).start()
    for p in order[1:]:
        load_lower(p).start()
    for l in range(1, lev):
        load_linv(l).start()
    for p in back:
        load_upper(p).start()
    for l in range(lev - 1, -1, -1):
        load_uinv(l).start()

    barrier = pltpu.get_barrier_semaphore()

    def greet(to_row, to_col):
        pl.semaphore_signal(barrier, inc=1, device_id=(to_row, to_col), device_id_type=MESH)

    each(nx, lambda k: greet(x_peer(k), c))
    each(nc, lambda k: greet(row, wrap(c + k, nc)))
    each(nz, lambda k: greet(z_peer(k), c))

    def greet_diagonal(cc):
        @pl.when(jnp.logical_not(jnp.logical_and(diagonal, cc == c)))
        def _():
            greet(c * nx + x, cc)

    def greet_run(k, carry):
        greet_diagonal(k)
        return carry

    lax.fori_loop(0, nc, greet_run, 0)

    lane = lax.broadcasted_iota(jnp.int32, (8, 128), 1)
    for t in range(nx):
        tile = jnp.zeros((8, 128), F32)
        for p in range(pairs):
            tile = jnp.where(lane == p, lower_fill[p, t, 0].astype(F32), tile)
            tile = jnp.where(lane == pairs + p, upper_fill[p, t, 0].astype(F32), tile)
        flag_out[t] = tile
    flag_x[x] = flag_out[x]

    pl.semaphore_wait(barrier, (nx - 1) + (nc - 1) + (nz - 1) + nc - diagonal.astype(jnp.int32))

    own_rows = pl.ds(pl.multiple_of(x * rows, rows), rows)

    def start_x(k):
        target = wrap(x + k, nx)
        send(flag_out.at[target], flag_x.at[x], fx_s, fx_r, x_peer(k), c)
        send(rhs.at[target], rhs_home.at[:, own_rows, :], rhs_s, rhs_r, x_peer(k), c)

    each(nx, start_x)
    pltpu.make_async_copy(rhs.at[x], rhs_home.at[:, own_rows, :], rhs_r).start()

    def chunk(index):
        return pl.ds(pl.multiple_of(index * step, step), step)

    def lower_to_columns(p):
        load_lower(p).wait()
        found = jnp.zeros((width, width), BF16)
        for t in range(nx):
            found = lax.select(lower_fill[p, t, 0] != 0, l_raw[p, t], found)
        l_loc[p] = found

        def go(k):
            peer = wrap(c + k, nc)
            send(l_loc.at[p, chunk(peer)], l_in.at[p, k - 1], ly_s.at[p], ly_r.at[p], row, peer)

        each(nc, go)

    def over_z(body):
        def run(zz, carry):
            same = jnp.logical_and(zz == z, diagonal)

            @pl.when(same)
            def _():
                body(zz, True)

            @pl.when(jnp.logical_not(same))
            def _():
                body(zz, False)

            return carry

        lax.fori_loop(0, nz, run, 0)

    def lower_to_home(p):
        wait(l_in.at[p], ly_r.at[p])
        total = l_loc[p, chunk(c), :]
        for k in range(nc - 1):
            total = total + l_in[p, k]
        l_sum[p] = total

        def go(zz, same):
            if same:
                pltpu.make_async_copy(l_sum.at[p], l_home.at[p, chunk(c)], ld_r.at[p]).start()
            else:
                send(
                    l_sum.at[p], l_home.at[p, chunk(c)], ld_s.at[p], ld_r.at[p],
                    zz * nx + x, z,
                )

        over_z(go)

    def flags_to_home():
        wait(flag_x.at[pl.ds(0, nx - 1)], fx_r)
        sub = lax.broadcasted_iota(jnp.int32, (8, 128), 0)
        tile = jnp.zeros((8, 128), F32)
        for k in range(nx):
            tile = jnp.where(sub == k, flag_x[k], tile)
        flag_row[...] = tile

        def go(zz, same):
            if same:
                pltpu.make_async_copy(flag_row, flag_all.at[c], fd_r).start()
            else:
                send(flag_row, flag_all.at[c], fd_s, fd_r, zz * nx + x, z)

        over_z(go)

    def flags_ready():
        wait(flag_all, fd_r)
        copy = pltpu.make_async_copy(flag_all, flags, flag_sem)
        copy.start()
        copy.wait()

    def upper_over_x(p):
        load_upper(p).wait()
        for t in range(nx):
            u_raw[p, t] = lax.select(
                upper_fill[p, t, 0] != 0, u_raw[p, t], jnp.zeros((width, width), BF16)
            )

        def go(k):
            send(u_raw.at[p, wrap(x + k, nx)], u_in.at[p, k - 1], ux_s.at[p], ux_r.at[p], x_peer(k), c)

        each(nx, go)

    def upper_over_z(p):
        wait(u_in.at[p], ux_r.at[p])
        total = u_raw[p, x]
        for k in range(nx - 1):
            total = total + u_in[p, k]
        u_sum[p] = total

        def go(k):
            send(
                u_sum.at[p, chunk(wrap(z + k, nz))], u_slice.at[p, k - 1], uz_s.at[p], uz_r.at[p],
                z_peer(k), c,
            )

        each(nz, go)

    def upper_to_all(p):
        wait(u_slice.at[p], uz_r.at[p])
        total = u_sum[p, chunk(z), :]
        for k in range(nz - 1):
            total = total + u_slice[p, k]
        u_home[p, chunk(z), :] = total

        def go(k):
            send(u_home.at[p, chunk(z)], u_home.at[p, chunk(z)], ua_s.at[p], ua_r.at[p], z_peer(k), c)

        each(nz, go)

    def product(left, right):
        return jnp.dot(left, right, preferred_element_type=F32)

    def contribute(a, b):
        p = pair_index(a, b)
        wait(l_home.at[p], ld_r.at[p])
        near[p, x] = product(fwd[b], l_home[p]).astype(BF16)
        each(nx, lambda k: send(near.at[p, x], near.at[p, x], na_s.at[p], na_r.at[p], x_peer(k), c))

    def mix(column, level):
        total = None
        for m in range(level):
            p = pair_index(level, m)
            for k in range(nx):
                term = near[p, k].astype(F32) * flags[column, k, p]
                total = term if total is None else total + term
        return total

    def spread_parts(level):
        for m in range(level):
            p = pair_index(level, m)
            wait(near.at[p, pl.ds(0, nx - 1)], na_r.at[p])

        def go(k):
            peer = wrap(c + k, nc)
            part_out[level - 1, k - 1] = mix(peer, level).astype(BF16)
            send(
                part_out.at[level - 1, k - 1], part_in.at[level - 1, k - 1],
                pb_s.at[level - 1], pb_r.at[level - 1], row, peer,
            )

        each(nc, go)

    def collect_parts(level):
        total = mix(c, level)
        wait(part_in.at[level - 1], pb_r.at[level - 1])
        for k in range(nc - 1):
            total = total + part_in[level - 1, k].astype(F32)
        return (rhs_home[level].astype(F32) - total).astype(BF16)

    def solve_lower(level, residual):
        load_linv(level).wait()
        fwd[level] = product(residual, linv[level]).astype(BF16)

    def solve_upper(level, residual):
        load_uinv(level).wait()
        result = product(residual, uinv[level])
        if level:
            solved[level, x] = result.astype(BF16)
            each(
                nx,
                lambda k: send(
                    solved.at[level, x], solved.at[level, x], xa_s.at[level], xa_r.at[level],
                    x_peer(k), c,
                ),
            )
        answer[level] = result

        def go(k):
            target = wrap(x + k, nx)
            there = pl.ds(pl.multiple_of(target * rows, rows), rows)
            send(answer.at[level, there], out.at[level, x], out_s.at[level], out_r.at[level], x_peer(k), c)

        each(nx, go)
        pltpu.make_async_copy(answer.at[level, own_rows], out.at[level, x], out_r.at[level]).start()

    def choose(column, a, p):
        total = None
        for k in range(nx):
            term = solved[a, k].astype(F32) * flags[column, k, pairs + p]
            total = term if total is None else total + term
        return total.astype(BF16)

    def solved_ready(a):
        wait(solved.at[a, pl.ds(0, nx - 1)], xa_r.at[a])

    def spread_solved(a, b):
        p = pair_index(a, b)

        def go(k):
            peer = wrap(c + k, nc)
            pick_out[p, k - 1] = choose(peer, a, p)
            send(
                pick_out.at[p, k - 1], pick_in.at[p, k - 1], xb_s.at[p], xb_r.at[p], row, peer
            )

        each(nc, go)
        pick_own[p] = choose(c, a, p)

    def gather_solved(a, b):
        p = pair_index(a, b)
        wait(pick_in.at[p], xb_r.at[p])
        source = pick_own[p]
        for k in range(nc - 1):
            source = source + pick_in[p, k]
        wait(u_home.at[p, pl.ds(0, width - step)], ua_r.at[p])
        return product(source, u_home[p])

    idx = pair_index
    for p in order:
        lower_to_columns(p)
    flags_to_home()
    wait(rhs_home, rhs_r)
    solve_lower(0, rhs_home[0])
    lower_to_home(idx(1, 0))
    upper_over_x(idx(3, 2))
    lower_to_home(idx(2, 0))
    lower_to_home(idx(2, 1))
    contribute(1, 0)
    flags_ready()
    for b in range(3):
        lower_to_home(idx(3, b))
    spread_parts(1)
    contribute(2, 0)
    upper_over_x(idx(2, 1))
    upper_over_z(idx(3, 2))
    solve_lower(1, collect_parts(1))
    contribute(2, 1)
    upper_over_x(idx(3, 1))
    spread_parts(2)
    contribute(3, 0)
    contribute(3, 1)
    upper_to_all(idx(3, 2))
    upper_over_z(idx(2, 1))
    solve_lower(2, collect_parts(2))
    contribute(3, 2)
    upper_over_x(idx(1, 0))
    spread_parts(3)
    upper_over_z(idx(3, 1))
    upper_to_all(idx(2, 1))
    solve_lower(3, collect_parts(3))
    solve_upper(3, fwd[3])
    upper_over_x(idx(2, 0))
    upper_over_z(idx(1, 0))
    upper_to_all(idx(3, 1))
    solved_ready(3)
    spread_solved(3, 2)
    spread_solved(3, 1)
    spread_solved(3, 0)
    upper_over_x(idx(3, 0))
    total = gather_solved(3, 2)
    solve_upper(2, (fwd[2].astype(F32) - total).astype(BF16))
    upper_over_z(idx(2, 0))
    upper_to_all(idx(1, 0))
    solved_ready(2)
    spread_solved(2, 1)
    spread_solved(2, 0)
    total = gather_solved(3, 1)
    total = total + gather_solved(2, 1)
    solve_upper(1, (fwd[1].astype(F32) - total).astype(BF16))
    upper_over_z(idx(3, 0))
    upper_to_all(idx(2, 0))
    solved_ready(1)
    spread_solved(1, 0)
    upper_to_all(idx(3, 0))
    total = gather_solved(3, 0)
    total = total + gather_solved(2, 0)
    total = total + gather_solved(1, 0)
    solve_upper(0, (fwd[0].astype(F32) - total).astype(BF16))

    for p in range(pairs):
        wait(l_in.at[p], ly_s.at[p])
        wait(u_in.at[p], ux_s.at[p])
        wait(u_slice.at[p], uz_s.at[p])
        wait(u_slice.at[p], ua_s.at[p])
        wait(near.at[p, pl.ds(0, nx - 1)], na_s.at[p])
        wait(pick_in.at[p], xb_s.at[p])
    for l in range(lev - 1):
        wait(part_in.at[l], pb_s.at[l])
        wait(solved.at[l + 1, pl.ds(0, nx - 1)], xa_s.at[l + 1])
    wait(flag_x.at[pl.ds(0, nx - 1)], fx_s)
    wait(rhs_home.at[pl.ds(0, nx - 1)] if lev == nx else rhs.at[pl.ds(0, nx - 1)], rhs_s)

    @pl.when(diagonal)
    def _():
        for p in range(pairs):
            wait(l_home.at[p, pl.ds(0, width - step)], ld_s.at[p])
        wait(flag_all.at[pl.ds(0, nz - 1)], fd_s)

    @pl.when(jnp.logical_not(diagonal))
    def _():
        for p in range(pairs):
            wait(l_home.at[p], ld_s.at[p])
        wait(flag_all, fd_s)

    for l in range(lev):
        wait(out.at[l, pl.ds(0, nx - 1)], out_s.at[l])
        wait(out.at[l], out_r.at[l])


def per_device(
    right_sides, lower_blocks, lower_fill, upper_blocks, upper_fill, lower_inv, upper_inv
):
    lev, rows, nx, width = right_sides.shape
    nc = lax.axis_size("col")
    pairs = lev * (lev - 1) // 2
    step = width // nc
    wide = rows * nx
    by_target = jnp.transpose(right_sides, (2, 0, 1, 3))

    def vmem(shape, dtype=BF16):
        return pltpu.VMEM(shape, dtype)

    def dma(*shape):
        return pltpu.SemaphoreType.DMA(shape)

    square = (width, width)
    block = (wide, width)
    scratch = [
        vmem((pairs, nx) + square),
        vmem((pairs, nx) + square),
        vmem((lev,) + square),
        vmem((lev,) + square),
        vmem((pairs,) + square),
        vmem((pairs, nc - 1, step, width)),
        vmem((pairs, step, width)),
        vmem((pairs,) + square),
        vmem((pairs, nx - 1) + square),
        vmem((pairs,) + square),
        vmem((pairs, nc - 1, step, width)),
        vmem((pairs,) + square),
        vmem((lev,) + block),
        vmem((lev,) + block),
        vmem((nx, 8, 128), F32),
        vmem((nx, 8, 128), F32),
        vmem((8, 128), F32),
        vmem((nc, 8, 128), F32),
        pltpu.SMEM((nc, 8, 128), F32),
        vmem((pairs, nx) + block),
        vmem((lev - 1, nc - 1) + block),
        vmem((lev - 1, nc - 1) + block),
        vmem((lev, nx) + block),
        vmem((pairs, nc - 1) + block),
        vmem((pairs, nc - 1) + block),
        vmem((pairs,) + block),
        vmem((lev,) + block, F32),
        dma(2 * pairs),
        dma(2 * lev),
        pltpu.SemaphoreType.DMA,
    ]
    scratch += [pltpu.SemaphoreType.DMA] * 6
    scratch += [dma(pairs)] * 12
    scratch += [dma(lev - 1)] * 2
    scratch += [dma(lev)] * 2
    scratch += [dma(pairs)] * 2
    scratch += [dma(lev)] * 2
    anywhere = pl.BlockSpec(memory_space=pl.ANY)
    scalars = pl.BlockSpec(memory_space=pltpu.SMEM)
    result = pl.pallas_call(
        functools.partial(sweep_kernel, (lev, nx, nc, rows, width)),
        out_shape=jax.ShapeDtypeStruct((lev, nx, rows, width), F32),
        in_specs=[anywhere, anywhere, scalars, anywhere, scalars, anywhere, anywhere],
        out_specs=anywhere,
        scratch_shapes=scratch,
        compiler_params=pltpu.CompilerParams(
            collective_id=0, has_side_effects=True, vmem_limit_bytes=48 * 1024 * 1024
        ),
    )(by_target, lower_blocks, lower_fill, upper_blocks, upper_fill, lower_inv, upper_inv)
    return jnp.transpose(result, (0, 2, 1, 3))


def solution(mesh):
    placed = (
        P(None, "row", "col", None),
        P(None, "col", "row", None, None),
        P(None, "col", "row"),
        P(None, "col", "row", None, None),
        P(None, "col", "row"),
        P(None, "col", None, None),
        P(None, "col", None, None),
    )
    return jax.shard_map(
        per_device,
        mesh=mesh,
        in_specs=placed,
        out_specs=P(None, "row", "col", None),
        check_vma=False,
    )
```

time: 1980 us -> 109 us (0.06)
  waiting for transfers between devices: 1900 us -> 0 us
  Pallas kernels: 0 us -> 103 us
  matrix products: 38.9 us -> 0 us
    reduce_scatter x3 -> x0, waiting for transfers between devices: 643 us -> none  [triangular_sweep(): lax.psum_scatter(partial_terms(jnp.int32(0), local_rows * lax.axis_size('...]
    unnamed x21 -> x0, waiting for transfers between devices: 452 us -> none
    all_gather x6 -> x0, waiting for transfers between devices: 416 us -> none  [deliver(): gathered = lax.all_gather(solved_local, 'row', axis=0, tiled=True)]
    psum x6 -> x0, waiting for transfers between devices: 388 us -> none  [spread(): return lax.psum(jnp.where(mine, x, jnp.zeros_like(x)), axis)]
    pallas_call x0 -> x1, Pallas kernels: none -> 103 us  [per_device(): pl.pallas_call(functools.partial(sweep_kernel, (lev, nx, nc, rows, width)...]
    dot_general x19 -> x0, matrix products: 38.9 us -> none  [the longest x12 26.6 us: partial_terms(): jnp.einsum('rv,tvw->rtw', solution_rows, block_tiles, preferred_element_t...]
  transfers between devices with their start and end apart: 18 -> 0, of which waited for: 18 -> 0; matrix products, arithmetic and copies ran while one was open for 1% -> 0% of each run, Pallas kernels for 0% -> 0%
where the time goes in v1:
time: 109 us
  Pallas kernels  103 us (94%)
  local copies, waits for them, and re-layouts  6.54 us (6%)
    pallas_call x1, Pallas kernels, per_device(): pl.pallas_call(functools.partial(sweep_kernel, (lev, nx, nc, rows, width)...  103 us
    unnamed x7, local copies, waits for them, and re-layouts  5.67 us

profile of v1, /device:TPU:1, one launch (start us, length us, event | category | flops | bytes accessed | tf_op | source)
XLA Modules:
  0.0 109.1 jit_solution(1251764095548874391)
XLA Ops:
  0.0 0.8 copy.9.lower_fill
  0.8 0.8 copy.10.upper_fill
  1.6 0.9 copy.13
  2.5 0.0 copy-start
  2.5 1.6 %copy-done = bf16[4,4,256,256]{3,2,1,0:T(8,128)(2,1)S(1)} copy-done((bf16[4,4,256,256]{3,2,1,0:T(8,128)(2,1)S(1)}, bf16[4,4,256,256]{3,2,1,0:T(8,128)(2,1)}, u32[]{:S(2)}) %copy-start) | copy-done | bytes 2097176
  4.1 0.0 copy-start.1
  4.1 1.6 %copy-done.1 = bf16[4,4,256,256]{3,2,1,0:T(8,128)(2,1)S(1)} copy-done((bf16[4,4,256,256]{3,2,1,0:T(8,128)(2,1)S(1)}, bf16[4,4,256,256]{3,2,1,0:T(8,128)(2,1)}, u32[]{:S(2)}) %copy-start.1) | copy-done | bytes 2097176
  5.7 102.5 %shard_map.73 = f32[4,4,16,256]{3,2,1,0:T(8,128)S(1)} custom-call(bf16[4,4,16,256]{3,2,1,0:T(8,128)(2,1)S(1)} %bitcast.5, bf16[6,4,1,256,256]{4,3,2,1,0:T(8,128)(2,1)} %lower.1, s32[6,4,1]{2,1,0:T(4,128)S(1)} %copy.9.lower_fill, bf16[6,4,1,256,256]{4,3,2,1,0:T(8,128)(2,1)} %upper.1, s32[6,4,1]{2,1,0:T(4,128)S(1)} %copy.10.upper_fill, ...), custom_call_target="tpu_custom_call" | custom-call | tf_op jit(solution)/shard_map/pallas_call | solution.py:497
  108.2 0.9 copy.11
Async XLA Ops:
  2.5 1.6 %copy-start = (bf16[4,4,256,256]{3,2,1,0:T(8,128)(2,1)S(1)}, bf16[4,4,256,256]{3,2,1,0:T(8,128)(2,1)}, u32[]{:S(2)}) copy-start(bf16[4,4,256,256]{3,2,1,0:T(8,128)(2,1)} %lower_inv.1) | copy-start | bytes 6291460
  4.1 1.6 %copy-start.1 = (bf16[4,4,256,256]{3,2,1,0:T(8,128)(2,1)S(1)}, bf16[4,4,256,256]{3,2,1,0:T(8,128)(2,1)}, u32[]{:S(2)}) copy-start(bf16[4,4,256,256]{3,2,1,0:T(8,128)(2,1)} %upper_inv.1) | copy-start | bytes 6291460

commit v2 on v1

--- a/solution.py
+++ b/solution.py
@@ -10,6 +10,7 @@
 MESH = pl.DeviceIdType.MESH
 F32 = jnp.float32
 BF16 = jnp.bfloat16
+PARTS = 2
 
 
 def pair_index(current, earlier):
@@ -19,15 +20,17 @@
 
 
 def sweep_kernel(
-    dims, rhs, lower, lower_fill, upper, upper_fill, lower_inv, upper_inv, out,
+    dims, rhs_raw, lower, lower_fill, upper, upper_fill, lower_inv, upper_inv, out,
     l_raw, u_raw, linv, uinv, l_loc, l_in, l_sum, l_home, u_in, u_sum, u_slice, u_home,
     rhs_home, fwd, flag_out, flag_x, flag_row, flag_all, flags,
+    rhs_tile, rhs, raw_sem,
     near, part_out, part_in, solved, pick_out, pick_in, pick_own, answer,
     load_sem, inv_sem, flag_sem,
     rhs_s, rhs_r, fx_s, fx_r, fd_s, fd_r, ly_s, ly_r, ld_s, ld_r, ux_s, ux_r, uz_s, uz_r,
     ua_s, ua_r, na_s, na_r, pb_s, pb_r, xa_s, xa_r, xb_s, xb_r, out_s, out_r,
 ):
-    lev, nx, nc, rows, width = dims
+    lev, nx, nc, rows, width, parts = dims
+    share = rows * nx // parts
     pairs = lev * (lev - 1) // 2
     nz = nc
     step = width // nc
@@ -83,13 +86,17 @@
     def load_uinv(l):
         return pltpu.make_async_copy(upper_inv.at[l, x], uinv.at[l], inv_sem.at[lev + l])
 
+    fetch = pltpu.make_async_copy(rhs_raw, rhs_tile, raw_sem)
+    fetch.start()
     load_lower(order[0]).start()
+    load_upper(back[0]).start()
     load_linv(0).start()
+    load_upper(back[1]).start()
     for p in order[1:]:
         load_lower(p).start()
     for l in range(1, lev):
         load_linv(l).start()
-    for p in back:
+    for p in back[2:]:
         load_upper(p).start()
     for l in range(lev - 1, -1, -1):
         load_uinv(l).start()
@@ -114,12 +121,17 @@
 
     lax.fori_loop(0, nc, greet_run, 0)
 
+    fetch.wait()
+    for l in range(lev):
+        for t in range(nx):
+            rhs[t, l] = rhs_tile[l, :, t, :]
+
     lane = lax.broadcasted_iota(jnp.int32, (8, 128), 1)
     for t in range(nx):
         tile = jnp.zeros((8, 128), F32)
         for p in range(pairs):
-            tile = jnp.where(lane == p, lower_fill[p, t, 0].astype(F32), tile)
-            tile = jnp.where(lane == pairs + p, upper_fill[p, t, 0].astype(F32), tile)
+            tile = jnp.where(lane == p, lower_fill[t, 0, p].astype(F32), tile)
+            tile = jnp.where(lane == pairs + p, upper_fill[t, 0, p].astype(F32), tile)
         flag_out[t] = tile
     flag_x[x] = flag_out[x]
 
@@ -142,7 +154,7 @@
         load_lower(p).wait()
         found = jnp.zeros((width, width), BF16)
         for t in range(nx):
-            found = lax.select(lower_fill[p, t, 0] != 0, l_raw[p, t], found)
+            found = lax.select(lower_fill[t, 0, p] != 0, l_raw[p, t], found)
         l_loc[p] = found
 
         def go(k):
@@ -211,7 +223,7 @@
         load_upper(p).wait()
         for t in range(nx):
             u_raw[p, t] = lax.select(
-                upper_fill[p, t, 0] != 0, u_raw[p, t], jnp.zeros((width, width), BF16)
+                upper_fill[t, 0, p] != 0, u_raw[p, t], jnp.zeros((width, width), BF16)
             )
 
         def go(k):
@@ -249,173 +261,239 @@
     def product(left, right):
         return jnp.dot(left, right, preferred_element_type=F32)
 
-    def contribute(a, b):
+    def over_parts(body):
+        def run(h, carry):
+            body(h)
+            return carry
+
+        lax.fori_loop(0, parts, run, 0)
+
+    def part_rows(h):
+        return pl.ds(pl.multiple_of(h * share, share), share)
+
+    def lower_ready(p):
+        wait(l_home.at[p], ld_r.at[p])
+
+    def contribute(h, a, b):
         p = pair_index(a, b)
-        wait(l_home.at[p], ld_r.at[p])
-        near[p, x] = product(fwd[b], l_home[p]).astype(BF16)
-        each(nx, lambda k: send(near.at[p, x], near.at[p, x], na_s.at[p], na_r.at[p], x_peer(k), c))
-
-    def mix(column, level):
+        near[h, p, x] = product(fwd[b, part_rows(h), :], l_home[p]).astype(BF16)
+
+        def go(k):
+            send(
+                near.at[h, p, x], near.at[h, p, x], na_s.at[h, p], na_r.at[h, p], x_peer(k), c
+            )
+
+        each(nx, go)
+
+    def mix(h, column, level):
         total = None
         for m in range(level):
             p = pair_index(level, m)
             for k in range(nx):
-                term = near[p, k].astype(F32) * flags[column, k, p]
+                term = near[h, p, k].astype(F32) * flags[column, k, p]
                 total = term if total is None else total + term
         return total
 
-    def spread_parts(level):
+    def spread_parts(h, level):
         for m in range(level):
             p = pair_index(level, m)
-            wait(near.at[p, pl.ds(0, nx - 1)], na_r.at[p])
+            wait(near.at[h, p, pl.ds(0, nx - 1)], na_r.at[h, p])
 
         def go(k):
             peer = wrap(c + k, nc)
-            part_out[level - 1, k - 1] = mix(peer, level).astype(BF16)
+            part_out[h, level - 1, k - 1] = mix(h, peer, level).astype(BF16)
             send(
-                part_out.at[level - 1, k - 1], part_in.at[level - 1, k - 1],
-                pb_s.at[level - 1], pb_r.at[level - 1], row, peer,
+                part_out.at[h, level - 1, k - 1], part_in.at[h, level - 1, k - 1],
+                pb_s.at[h, level - 1], pb_r.at[h, level - 1], row, peer,
             )
 
         each(nc, go)
 
-    def collect_parts(level):
-        total = mix(c, level)
-        wait(part_in.at[level - 1], pb_r.at[level - 1])
+    def collect_parts(h, level):
+        total = mix(h, c, level)
+        wait(part_in.at[h, level - 1], pb_r.at[h, level - 1])
         for k in range(nc - 1):
-            total = total + part_in[level - 1, k].astype(F32)
-        return (rhs_home[level].astype(F32) - total).astype(BF16)
-
-    def solve_lower(level, residual):
-        load_linv(level).wait()
-        fwd[level] = product(residual, linv[level]).astype(BF16)
-
-    def solve_upper(level, residual):
-        load_uinv(level).wait()
+            total = total + part_in[h, level - 1, k].astype(F32)
+        return (rhs_home[level, part_rows(h), :].astype(F32) - total).astype(BF16)
+
+    def solve_lower(h, level, residual):
+        fwd[level, part_rows(h), :] = product(residual, linv[level]).astype(BF16)
+
+    def solve_upper(h, level, residual):
         result = product(residual, uinv[level])
         if level:
-            solved[level, x] = result.astype(BF16)
-            each(
-                nx,
-                lambda k: send(
-                    solved.at[level, x], solved.at[level, x], xa_s.at[level], xa_r.at[level],
-                    x_peer(k), c,
-                ),
-            )
-        answer[level] = result
-
+            solved[h, level, x] = result.astype(BF16)
+
+            def go(k):
+                send(
+                    solved.at[h, level, x], solved.at[h, level, x],
+                    xa_s.at[h, level], xa_r.at[h, level], x_peer(k), c,
+                )
+
+            each(nx, go)
+        answer[level, part_rows(h), :] = result
+
+    def give_answer(level):
         def go(k):
             target = wrap(x + k, nx)
             there = pl.ds(pl.multiple_of(target * rows, rows), rows)
-            send(answer.at[level, there], out.at[level, x], out_s.at[level], out_r.at[level], x_peer(k), c)
+            send(
+                answer.at[level, there], out.at[level, x], out_s.at[level], out_r.at[level],
+                x_peer(k), c,
+            )
 
         each(nx, go)
         pltpu.make_async_copy(answer.at[level, own_rows], out.at[level, x], out_r.at[level]).start()
 
-    def choose(column, a, p):
+    def choose(h, column, a, p):
         total = None
         for k in range(nx):
-            term = solved[a, k].astype(F32) * flags[column, k, pairs + p]
+            term = solved[h, a, k].astype(F32) * flags[column, k, pairs + p]
             total = term if total is None else total + term
         return total.astype(BF16)
 
-    def solved_ready(a):
-        wait(solved.at[a, pl.ds(0, nx - 1)], xa_r.at[a])
-
-    def spread_solved(a, b):
+    def solved_ready(h, a):
+        wait(solved.at[h, a, pl.ds(0, nx - 1)], xa_r.at[h, a])
+
+    def spread_solved(h, a, b):
         p = pair_index(a, b)
 
         def go(k):
             peer = wrap(c + k, nc)
-            pick_out[p, k - 1] = choose(peer, a, p)
+            pick_out[h, p, k - 1] = choose(h, peer, a, p)
             send(
-                pick_out.at[p, k - 1], pick_in.at[p, k - 1], xb_s.at[p], xb_r.at[p], row, peer
+                pick_out.at[h, p, k - 1], pick_in.at[h, p, k - 1],
+                xb_s.at[h, p], xb_r.at[h, p], row, peer,
             )
 
         each(nc, go)
-        pick_own[p] = choose(c, a, p)
-
-    def gather_solved(a, b):
+        pick_own[h, p] = choose(h, c, a, p)
+
+    def upper_ready(p):
+        wait(u_home.at[p, pl.ds(0, width - step)], ua_r.at[p])
+
+    def gather_solved(h, a, b):
         p = pair_index(a, b)
-        wait(pick_in.at[p], xb_r.at[p])
-        source = pick_own[p]
+        wait(pick_in.at[h, p], xb_r.at[h, p])
+        source = pick_own[h, p]
         for k in range(nc - 1):
-            source = source + pick_in[p, k]
-        wait(u_home.at[p, pl.ds(0, width - step)], ua_r.at[p])
+            source = source + pick_in[h, p, k]
         return product(source, u_home[p])
 
+    def first_level(h):
+        solve_lower(h, 0, rhs_home[0, part_rows(h), :])
+
+    def next_level(level):
+        load_linv(level).wait()
+        lower_ready(pair_index(level + 1, level))
+
+        def body(h):
+            solve_lower(h, level, collect_parts(h, level))
+            contribute(h, level + 1, level)
+
+        over_parts(body)
+
+    def back_level(level):
+        load_uinv(level).wait()
+        for a in range(level + 1, lev):
+            upper_ready(pair_index(a, level))
+
+        def body(h):
+            total = None
+            for a in range(lev - 1, level, -1):
+                term = gather_solved(h, a, level)
+                total = term if total is None else total + term
+            residual = (fwd[level, part_rows(h), :].astype(F32) - total).astype(BF16)
+            solve_upper(h, level, residual)
+
+        over_parts(body)
+        give_answer(level)
+
+    def turn(h):
+        solve_lower(h, 3, collect_parts(h, 3))
+        solve_upper(h, 3, fwd[3, part_rows(h), :])
+
+    def pass_up(a, b):
+        lower_ready(pair_index(a, b))
+        over_parts(lambda h: contribute(h, a, b))
+
+    def pass_down(a, b, arrived=False):
+        def body(h):
+            if arrived:
+                solved_ready(h, a)
+            spread_solved(h, a, b)
+
+        over_parts(body)
+
     idx = pair_index
-    for p in order:
-        lower_to_columns(p)
+    lower_to_columns(idx(1, 0))
+    upper_over_x(idx(3, 2))
     flags_to_home()
     wait(rhs_home, rhs_r)
-    solve_lower(0, rhs_home[0])
+    load_linv(0).wait()
+    over_parts(first_level)
     lower_to_home(idx(1, 0))
-    upper_over_x(idx(3, 2))
+    lower_to_columns(idx(2, 0))
+    lower_to_columns(idx(2, 1))
+    upper_over_x(idx(2, 1))
     lower_to_home(idx(2, 0))
     lower_to_home(idx(2, 1))
-    contribute(1, 0)
+    pass_up(1, 0)
     flags_ready()
     for b in range(3):
+        lower_to_columns(idx(3, b))
+    upper_over_z(idx(3, 2))
+    over_parts(lambda h: spread_parts(h, 1))
+    upper_over_x(idx(3, 1))
+    next_level(1)
+    for b in range(3):
         lower_to_home(idx(3, b))
-    spread_parts(1)
-    contribute(2, 0)
-    upper_over_x(idx(2, 1))
-    upper_over_z(idx(3, 2))
-    solve_lower(1, collect_parts(1))
-    contribute(2, 1)
-    upper_over_x(idx(3, 1))
-    spread_parts(2)
-    contribute(3, 0)
-    contribute(3, 1)
+    pass_up(2, 0)
+    upper_over_z(idx(2, 1))
+    over_parts(lambda h: spread_parts(h, 2))
+    upper_over_x(idx(1, 0))
     upper_to_all(idx(3, 2))
-    upper_over_z(idx(2, 1))
-    solve_lower(2, collect_parts(2))
-    contribute(3, 2)
-    upper_over_x(idx(1, 0))
-    spread_parts(3)
+    next_level(2)
+    pass_up(3, 0)
+    pass_up(3, 1)
     upper_over_z(idx(3, 1))
     upper_to_all(idx(2, 1))
-    solve_lower(3, collect_parts(3))
-    solve_upper(3, fwd[3])
+    over_parts(lambda h: spread_parts(h, 3))
     upper_over_x(idx(2, 0))
+    load_linv(3).wait()
+    load_uinv(3).wait()
+    over_parts(turn)
+    give_answer(3)
     upper_over_z(idx(1, 0))
     upper_to_all(idx(3, 1))
-    solved_ready(3)
-    spread_solved(3, 2)
-    spread_solved(3, 1)
-    spread_solved(3, 0)
+    pass_down(3, 2, True)
     upper_over_x(idx(3, 0))
-    total = gather_solved(3, 2)
-    solve_upper(2, (fwd[2].astype(F32) - total).astype(BF16))
+    pass_down(3, 1)
     upper_over_z(idx(2, 0))
+    back_level(2)
     upper_to_all(idx(1, 0))
-    solved_ready(2)
-    spread_solved(2, 1)
-    spread_solved(2, 0)
-    total = gather_solved(3, 1)
-    total = total + gather_solved(2, 1)
-    solve_upper(1, (fwd[1].astype(F32) - total).astype(BF16))
+    pass_down(2, 1, True)
+    pass_down(3, 0)
     upper_over_z(idx(3, 0))
     upper_to_all(idx(2, 0))
-    solved_ready(1)
-    spread_solved(1, 0)
+    back_level(1)
+    pass_down(2, 0)
     upper_to_all(idx(3, 0))
-    total = gather_solved(3, 0)
-    total = total + gather_solved(2, 0)
-    total = total + gather_solved(1, 0)
-    solve_upper(0, (fwd[0].astype(F32) - total).astype(BF16))
+    pass_down(1, 0, True)
+    back_level(0)
 
     for p in range(pairs):
         wait(l_in.at[p], ly_s.at[p])
         wait(u_in.at[p], ux_s.at[p])
         wait(u_slice.at[p], uz_s.at[p])
         wait(u_slice.at[p], ua_s.at[p])
-        wait(near.at[p, pl.ds(0, nx - 1)], na_s.at[p])
-        wait(pick_in.at[p], xb_s.at[p])
+        for h in range(parts):
+            wait(near.at[h, p, pl.ds(0, nx - 1)], na_s.at[h, p])
+            wait(pick_in.at[h, p], xb_s.at[h, p])
     for l in range(lev - 1):
-        wait(part_in.at[l], pb_s.at[l])
-        wait(solved.at[l + 1, pl.ds(0, nx - 1)], xa_s.at[l + 1])
+        for h in range(parts):
+            wait(part_in.at[h, l], pb_s.at[h, l])
+            wait(solved.at[h, l + 1, pl.ds(0, nx - 1)], xa_s.at[h, l + 1])
     wait(flag_x.at[pl.ds(0, nx - 1)], fx_s)
     wait(rhs_home.at[pl.ds(0, nx - 1)] if lev == nx else rhs.at[pl.ds(0, nx - 1)], rhs_s)
 
@@ -444,7 +522,6 @@
     pairs = lev * (lev - 1) // 2
     step = width // nc
     wide = rows * nx
-    by_target = jnp.transpose(right_sides, (2, 0, 1, 3))
 
     def vmem(shape, dtype=BF16):
         return pltpu.VMEM(shape, dtype)
@@ -454,6 +531,7 @@
 
     square = (width, width)
     block = (wide, width)
+    part = (wide // PARTS, width)
     scratch = [
         vmem((pairs, nx) + square),
         vmem((pairs, nx) + square),
@@ -474,36 +552,43 @@
         vmem((8, 128), F32),
         vmem((nc, 8, 128), F32),
         pltpu.SMEM((nc, 8, 128), F32),
-        vmem((pairs, nx) + block),
-        vmem((lev - 1, nc - 1) + block),
-        vmem((lev - 1, nc - 1) + block),
-        vmem((lev, nx) + block),
-        vmem((pairs, nc - 1) + block),
-        vmem((pairs, nc - 1) + block),
-        vmem((pairs,) + block),
+        vmem((lev, rows, nx, width)),
+        vmem((nx, lev, rows, width)),
+        pltpu.SemaphoreType.DMA,
+        vmem((PARTS, pairs, nx) + part),
+        vmem((PARTS, lev - 1, nc - 1) + part),
+        vmem((PARTS, lev - 1, nc - 1) + part),
+        vmem((PARTS, lev, nx) + part),
+        vmem((PARTS, pairs, nc - 1) + part),
+        vmem((PARTS, pairs, nc - 1) + part),
+        vmem((PARTS, pairs) + part),
         vmem((lev,) + block, F32),
         dma(2 * pairs),
         dma(2 * lev),
         pltpu.SemaphoreType.DMA,
     ]
     scratch += [pltpu.SemaphoreType.DMA] * 6
-    scratch += [dma(pairs)] * 12
-    scratch += [dma(lev - 1)] * 2
-    scratch += [dma(lev)] * 2
-    scratch += [dma(pairs)] * 2
+    scratch += [dma(pairs)] * 10
+    scratch += [dma(PARTS, pairs)] * 2
+    scratch += [dma(PARTS, lev - 1)] * 2
+    scratch += [dma(PARTS, lev)] * 2
+    scratch += [dma(PARTS, pairs)] * 2
     scratch += [dma(lev)] * 2
     anywhere = pl.BlockSpec(memory_space=pl.ANY)
     scalars = pl.BlockSpec(memory_space=pltpu.SMEM)
     result = pl.pallas_call(
-        functools.partial(sweep_kernel, (lev, nx, nc, rows, width)),
+        functools.partial(sweep_kernel, (lev, nx, nc, rows, width, PARTS)),
         out_shape=jax.ShapeDtypeStruct((lev, nx, rows, width), F32),
         in_specs=[anywhere, anywhere, scalars, anywhere, scalars, anywhere, anywhere],
         out_specs=anywhere,
         scratch_shapes=scratch,
         compiler_params=pltpu.CompilerParams(
-            collective_id=0, has_side_effects=True, vmem_limit_bytes=48 * 1024 * 1024
+            collective_id=0, has_side_effects=True, vmem_limit_bytes=60 * 1024 * 1024
         ),
-    )(by_target, lower_blocks, lower_fill, upper_blocks, upper_fill, lower_inv, upper_inv)
+    )(
+        right_sides, lower_blocks, jnp.transpose(lower_fill, (1, 2, 0)),
+        upper_blocks, jnp.transpose(upper_fill, (1, 2, 0)), lower_inv, upper_inv,
+    )
     return jnp.transpose(result, (0, 2, 1, 3))
 
 

time: 109 us -> 95.7 us (0.88)
  Pallas kernels: 103 us -> 93.8 us
  local copies, waits for them, and re-layouts: 6.54 us -> 1.82 us
    pallas_call x1, Pallas kernels: 103 us -> 93.8 us  [per_device(): pl.pallas_call(functools.partial(sweep_kernel, (lev, nx, nc, rows, width,...]
    unnamed x7 -> x0, local copies, waits for them, and re-layouts: 5.67 us -> none
where the time goes in v2:
time: 95.7 us; the launch traced here: 95.6 us
  Pallas kernels  93.8 us (98%)
  local copies, waits for them, and re-layouts  1.82 us (2%)
    pallas_call x1, Pallas kernels, per_device(): pl.pallas_call(functools.partial(sweep_kernel, (lev, nx, nc, rows, width,...  93.8 us

profile of v2, /device:TPU:1, one launch (start us, length us, event | category | flops | bytes accessed | tf_op | source)
XLA Modules:
  0.0 95.6 jit_solution(5487924650824531802)
XLA Ops:
  0.0 93.8 %shard_map.73 = f32[4,4,16,256]{3,2,1,0:T(8,128)} custom-call(bf16[4,16,4,256]{3,2,1,0:T(4,128)(2,1)} %rhs_raw.1, bf16[6,4,1,256,256]{4,3,2,1,0:T(8,128)(2,1)} %lower.1, s32[4,1,6]{2,1,0:T(1,128)} %bitcast.4, bf16[6,4,1,256,256]{4,3,2,1,0:T(8,128)(2,1)} %upper.1, s32[4,1,6]{2,1,0:T(1,128)} %bitcast.5, bf16[4,4,256,256]{3,2,1,0:T(8,128)(2,1)} %lower_inv.1, ...), custom_call_target="tpu_custom_call" | custom-call | tf_op jit(solution)/shard_map/pallas_call | solution.py:579
  93.8 1.8 %copy.8 = f32[4,16,4,256]{3,2,1,0:T(4,128)} copy(f32[4,16,4,256]{3,1,2,0:T(8,128)} %bitcast.3) | data formatting | bytes 524288 | tf_op jit(solution)/shard_map/transpose | solution.py:592

commit v3 on v2

--- a/solution.py
+++ b/solution.py
@@ -345,6 +345,22 @@
         each(nx, go)
         pltpu.make_async_copy(answer.at[level, own_rows], out.at[level, x], out_r.at[level]).start()
 
+    def give_part(h):
+        for u in range(nx // parts):
+            target = h * (nx // parts) + u
+            there = pl.ds(pl.multiple_of(target * rows, rows), rows)
+
+            @pl.when(target == x)
+            def _():
+                pltpu.make_async_copy(answer.at[0, there], out.at[0, x], out_r.at[0]).start()
+
+            @pl.when(target != x)
+            def _():
+                send(
+                    answer.at[0, there], out.at[0, x], out_s.at[0], out_r.at[0],
+                    z * nx + target, c,
+                )
+
     def choose(h, column, a, p):
         total = None
         for k in range(nx):
@@ -405,9 +421,12 @@
                 total = term if total is None else total + term
             residual = (fwd[level, part_rows(h), :].astype(F32) - total).astype(BF16)
             solve_upper(h, level, residual)
+            if not level:
+                give_part(h)
 
         over_parts(body)
-        give_answer(level)
+        if level:
+            give_answer(level)
 
     def turn(h):
         solve_lower(h, 3, collect_parts(h, 3))
@@ -435,19 +454,20 @@
     lower_to_home(idx(1, 0))
     lower_to_columns(idx(2, 0))
     lower_to_columns(idx(2, 1))
+    for b in range(3):
+        lower_to_columns(idx(3, b))
     upper_over_x(idx(2, 1))
     lower_to_home(idx(2, 0))
     lower_to_home(idx(2, 1))
     pass_up(1, 0)
+    lower_to_home(idx(3, 0))
     flags_ready()
-    for b in range(3):
-        lower_to_columns(idx(3, b))
     upper_over_z(idx(3, 2))
     over_parts(lambda h: spread_parts(h, 1))
     upper_over_x(idx(3, 1))
     next_level(1)
-    for b in range(3):
-        lower_to_home(idx(3, b))
+    lower_to_home(idx(3, 1))
+    lower_to_home(idx(3, 2))
     pass_up(2, 0)
     upper_over_z(idx(2, 1))
     over_parts(lambda h: spread_parts(h, 2))

time: 95.7 us -> 92 us (0.961)
  Pallas kernels: 93.8 us -> 90.1 us
    pallas_call x1, Pallas kernels: 93.8 us -> 90.1 us  [per_device(): pl.pallas_call(functools.partial(sweep_kernel, (lev, nx, nc, rows, width,...]
where the time goes in v3:
time: 92 us; the launch traced here: 91.9 us
  Pallas kernels  90.1 us (98%)
  local copies, waits for them, and re-layouts  1.82 us (2%)
    pallas_call x1, Pallas kernels, per_device(): pl.pallas_call(functools.partial(sweep_kernel, (lev, nx, nc, rows, width,...  90.1 us

profile of v3, /device:TPU:1, one launch (start us, length us, event | category | flops | bytes accessed | tf_op | source)
XLA Modules:
  0.0 91.9 jit_solution(13333625402627947016)
XLA Ops:
  0.0 90.1 %shard_map.73 = f32[4,4,16,256]{3,2,1,0:T(8,128)} custom-call(bf16[4,16,4,256]{3,2,1,0:T(4,128)(2,1)} %rhs_raw.1, bf16[6,4,1,256,256]{4,3,2,1,0:T(8,128)(2,1)} %lower.1, s32[4,1,6]{2,1,0:T(1,128)} %bitcast.4, bf16[6,4,1,256,256]{4,3,2,1,0:T(8,128)(2,1)} %upper.1, s32[4,1,6]{2,1,0:T(1,128)} %bitcast.5, bf16[4,4,256,256]{3,2,1,0:T(8,128)(2,1)} %lower_inv.1, ...), custom_call_target="tpu_custom_call" | custom-call | tf_op jit(solution)/shard_map/pallas_call | solution.py:599
  90.1 1.8 %copy.8 = f32[4,16,4,256]{3,2,1,0:T(4,128)} copy(f32[4,16,4,256]{3,1,2,0:T(8,128)} %bitcast.3) | data formatting | bytes 524288 | tf_op jit(solution)/shard_map/transpose | solution.py:612

commit v4 on v3

--- a/solution.py
+++ b/solution.py
@@ -86,6 +86,26 @@
     def load_uinv(l):
         return pltpu.make_async_copy(upper_inv.at[l, x], uinv.at[l], inv_sem.at[lev + l])
 
+    barrier = pltpu.get_barrier_semaphore()
+
+    def greet(to_row, to_col):
+        pl.semaphore_signal(barrier, inc=1, device_id=(to_row, to_col), device_id_type=MESH)
+
+
+    def greet_diagonal(cc):
+        @pl.when(jnp.logical_not(jnp.logical_and(diagonal, cc == c)))
+        def _():
+            greet(c * nx + x, cc)
+
+    def greet_run(k, carry):
+        greet_diagonal(k)
+        return carry
+
+    lax.fori_loop(0, nc, greet_run, 0)
+    each(nz, lambda k: greet(z_peer(k), c))
+    each(nc, lambda k: greet(row, wrap(c + k, nc)))
+    each(nx, lambda k: greet(x_peer(k), c))
+
     fetch = pltpu.make_async_copy(rhs_raw, rhs_tile, raw_sem)
     fetch.start()
     load_lower(order[0]).start()
@@ -101,26 +121,6 @@
     for l in range(lev - 1, -1, -1):
         load_uinv(l).start()
 
-    barrier = pltpu.get_barrier_semaphore()
-
-    def greet(to_row, to_col):
-        pl.semaphore_signal(barrier, inc=1, device_id=(to_row, to_col), device_id_type=MESH)
-
-    each(nx, lambda k: greet(x_peer(k), c))
-    each(nc, lambda k: greet(row, wrap(c + k, nc)))
-    each(nz, lambda k: greet(z_peer(k), c))
-
-    def greet_diagonal(cc):
-        @pl.when(jnp.logical_not(jnp.logical_and(diagonal, cc == c)))
-        def _():
-            greet(c * nx + x, cc)
-
-    def greet_run(k, carry):
-        greet_diagonal(k)
-        return carry
-
-    lax.fori_loop(0, nc, greet_run, 0)
-
     fetch.wait()
     for l in range(lev):
         for t in range(nx):
@@ -452,19 +452,19 @@
     load_linv(0).wait()
     over_parts(first_level)
     lower_to_home(idx(1, 0))
+    lower_to_columns(idx(2, 1))
     lower_to_columns(idx(2, 0))
-    lower_to_columns(idx(2, 1))
     for b in range(3):
         lower_to_columns(idx(3, b))
     upper_over_x(idx(2, 1))
-    lower_to_home(idx(2, 0))
     lower_to_home(idx(2, 1))
     pass_up(1, 0)
+    lower_to_home(idx(2, 0))
     lower_to_home(idx(3, 0))
     flags_ready()
+    upper_over_x(idx(3, 1))
     upper_over_z(idx(3, 2))
     over_parts(lambda h: spread_parts(h, 1))
-    upper_over_x(idx(3, 1))
     next_level(1)
     lower_to_home(idx(3, 1))
     lower_to_home(idx(3, 2))

time: 92 us -> 91.6 us (level)
  no operation moved by 1% of the time
where the time goes in v4:
time: 91.6 us; the launch traced here: 91.4 us
  Pallas kernels  89.6 us (98%)
  local copies, waits for them, and re-layouts  1.82 us (2%)
    pallas_call x1, Pallas kernels, per_device(): pl.pallas_call(functools.partial(sweep_kernel, (lev, nx, nc, rows, width,...  89.6 us

profile of v4, /device:TPU:1, one launch (start us, length us, event | category | flops | bytes accessed | tf_op | source)
XLA Modules:
  0.0 91.4 jit_solution(15485112582538785089)
XLA Ops:
  0.0 89.6 %shard_map.73 = f32[4,4,16,256]{3,2,1,0:T(8,128)} custom-call(bf16[4,16,4,256]{3,2,1,0:T(4,128)(2,1)} %rhs_raw.1, bf16[6,4,1,256,256]{4,3,2,1,0:T(8,128)(2,1)} %lower.1, s32[4,1,6]{2,1,0:T(1,128)} %bitcast.4, bf16[6,4,1,256,256]{4,3,2,1,0:T(8,128)(2,1)} %upper.1, s32[4,1,6]{2,1,0:T(1,128)} %bitcast.5, bf16[4,4,256,256]{3,2,1,0:T(8,128)(2,1)} %lower_inv.1, ...), custom_call_target="tpu_custom_call" | custom-call | tf_op jit(solution)/shard_map/pallas_call | solution.py:599
  89.6 1.8 %copy.8 = f32[4,16,4,256]{3,2,1,0:T(4,128)} copy(f32[4,16,4,256]{3,1,2,0:T(8,128)} %bitcast.3) | data formatting | bytes 524288 | tf_op jit(solution)/shard_map/transpose | solution.py:612

commit v5 on v4

--- a/solution.py
+++ b/solution.py
@@ -466,9 +466,9 @@
     upper_over_z(idx(3, 2))
     over_parts(lambda h: spread_parts(h, 1))
     next_level(1)
+    pass_up(2, 0)
+    lower_to_home(idx(3, 2))
     lower_to_home(idx(3, 1))
-    lower_to_home(idx(3, 2))
-    pass_up(2, 0)
     upper_over_z(idx(2, 1))
     over_parts(lambda h: spread_parts(h, 2))
     upper_over_x(idx(1, 0))

time: 91.6 us -> 92.2 us (level)
  no operation moved by 1% of the time
where the time goes in v5:
time: 92.2 us; the launch traced here: 92.1 us
  Pallas kernels  90.3 us (98%)
  local copies, waits for them, and re-layouts  1.82 us (2%)
    pallas_call x1, Pallas kernels, per_device(): pl.pallas_call(functools.partial(sweep_kernel, (lev, nx, nc, rows, width,...  90.3 us

profile of v5, /device:TPU:1, one launch (start us, length us, event | category | flops | bytes accessed | tf_op | source)
XLA Modules:
  0.0 92.1 jit_solution(14296150258169978609)
XLA Ops:
  0.0 90.3 %shard_map.73 = f32[4,4,16,256]{3,2,1,0:T(8,128)} custom-call(bf16[4,16,4,256]{3,2,1,0:T(4,128)(2,1)} %rhs_raw.1, bf16[6,4,1,256,256]{4,3,2,1,0:T(8,128)(2,1)} %lower.1, s32[4,1,6]{2,1,0:T(1,128)} %bitcast.4, bf16[6,4,1,256,256]{4,3,2,1,0:T(8,128)(2,1)} %upper.1, s32[4,1,6]{2,1,0:T(1,128)} %bitcast.5, bf16[4,4,256,256]{3,2,1,0:T(8,128)(2,1)} %lower_inv.1, ...), custom_call_target="tpu_custom_call" | custom-call | tf_op jit(solution)/shard_map/pallas_call | solution.py:599
  90.3 1.8 %copy.8 = f32[4,16,4,256]{3,2,1,0:T(4,128)} copy(f32[4,16,4,256]{3,1,2,0:T(8,128)} %bitcast.3) | data formatting | bytes 524288 | tf_op jit(solution)/shard_map/transpose | solution.py:612
